TPU v7x, 512 devices: a whole 4x4x16 slice. The times are simulated.
512 devices in a mesh: dp: 64 (over z, x_hi, core), rep: 8 (over y, x_lo).
Axes of the slice: x: 4 (x_hi: 2, x_lo: 2; x = x_hi * 2 + x_lo), y: 4, z: 16, core: 2. Of those that a mesh axis runs over, the one named last changes fastest.
Arguments:
- grad_out: bfloat16 [49152, 2048], P('dp', 'rep'), may hold values from -16 to 16
- pre_act: bfloat16 [49152, 3072], P('dp', 'rep'), may hold values from -6 to 6
- up_weight: bfloat16 [3072, 2048], P('rep'), may hold values from -0.125 to 0.125
- down_weight: bfloat16 [2048, 3072], P(None, 'rep'), may hold values from -0.109375 to 0.109375
- slot_counts: int32 [64], P('dp'), may hold values from 384 to 768, as said below
Outputs:
- input_grad: bfloat16 [49152, 2048], P('dp')
- down_grad: float32 [2048, 3072], P('dp', 'rep')
Inputs may be any that keep to these rules, and one draw needn't show every extreme that they name: Row i * 768 + j is live exactly when j < slot_counts[i]; some index has all 768 slots live and some index exactly 384.
All inputs are finite; a program needn't handle non-finite values.
Results may differ from a plain program's by a relative error of at most 0.0049.
Values may be sent and summed in bfloat16 or wider, within the bound.
No kernel may reach another device: no remote copies, remote signals or barrier semaphores. Data moves between devices by JAX's collectives and lax.ppermute only.
A program may use at most 64 MiB of HBM per device.

v0:
```python
import jax
import jax.numpy as jnp
from jax import lax
from jax.sharding import Mesh
from jax.sharding import PartitionSpec as P

REP = ("rep_0", "rep_1")


def whole_of(array, axes, dim):
    if not axes:
        return array
    nearer = lax.all_gather(array, axes[-1], axis=dim, tiled=True)
    return whole_of(nearer, axes[:-1], dim)


def on_device(grad_out, pre_act, up_weight, down_weight, slot_counts):
    slot_rows = grad_out.shape[0]
    live_rows = (lax.iota(jnp.int32, slot_rows) < slot_counts[0])[:, None]
    grad_full = whole_of(grad_out, REP, 1)
    grad_live = jnp.where(live_rows, grad_full, jnp.zeros_like(grad_full))
    zero_pre = jnp.zeros_like(pre_act)
    hidden = jnp.where(live_rows, jnp.maximum(pre_act, zero_pre), zero_pre)
    data_ranks = lax.axis_size("dp")
    down_sum = lax.psum_scatter(
        lax.dot_general(
            grad_live, hidden, (((0,), (0,)), ((), ())), preferred_element_type=jnp.float32
        ),
        "dp",
        scatter_dimension=0,
        tiled=True,
    )
    down_grad = down_sum / data_ranks
    hidden_grad = jnp.dot(grad_live, down_weight, preferred_element_type=jnp.float32)
    pre_grad = jnp.where(pre_act > 0, hidden_grad, jnp.zeros_like(hidden_grad)).astype(jnp.bfloat16)
    partial_terms = jnp.dot(pre_grad, up_weight, preferred_element_type=jnp.float32)
    input_sum = lax.psum(partial_terms, REP)
    input_grad = input_sum.astype(jnp.bfloat16)
    return (input_grad, down_grad)


def solution(mesh):
    finer = Mesh(mesh.devices.reshape(mesh.shape["dp"], 4, 2), ("dp", "rep_0", "rep_1"))
    in_specs = (P("dp", REP), P("dp", REP), P(REP, None), P(None, REP), P("dp"))
    out_specs = (P("dp", None), P("dp", REP))
    return jax.shard_map(
        on_device, mesh=finer, in_specs=in_specs, out_specs=out_specs, check_vma=False
    )
```

profile of v0, /device:TPU:4, one launch (start us, length us, event | category | flops | bytes accessed | tf_op | source)
XLA Modules:
  0.0 350.7 jit_solution(8490427789314710554)
XLA Ops:
  7.2 0.0 copy-start
  7.2 0.0 all-gather.2.cloned.1.call-start
  7.2 13.1 %all_gather.6 = bf16[768,512]{1,0:T(8,128)(2,1)} all-gather(bf16[768,256]{1,0:T(8,128)(2,1)} %param.5), channel_id=1, replica_groups=mesh['dp'=64,'rep_0'=4,'rep_1'=2] {'rep_1'}, dimensions={1}, use_global_device_ids=true | all-gather | bytes 1179648 | tf_op jit(solution)/shard_map/all_gather | solution.py:13
  20.3 0.0 all-gather.2.cloned.1.call-update
  20.4 0.0 reduce-scatter.2.cloned.1.call-start
  21.1 51.1 %all-gather.2.cloned.1.call-done = bf16[768,2048]{1,0:T(8,128)(2,1)} async-done(((bf16[768,512]{1,0:T(8,128)(2,1)}), bf16[768,2048]{1,0:T(8,128)(2,1)}) %all-gather.2.cloned.1.call-update) | async-done | bytes 3145744 | tf_op jit(solution)/shard_map/all_gather | solution.py:13
  72.2 5.6 %fusion.1 = f32[2048,384]{1,0:T(8,128)} fusion(bf16[768,2048]{1,0:T(8,128)(2,1)} %all-gather.2.cloned.1.call-done, pred[768]{0:T(1024)(128)(4,1)S(1)} %iota_compare_fusion, bf16[768,384]{1,0:T(8,128)(2,1)} %param.6), kind=kOutput, calls=%fused_computation.3 | convolution fusion | flops 1210122240 | bytes 6882048 | tf_op jit(solution)/shard_map/dot_general | solution.py:26
  77.8 0.0 copy-start.1
  77.8 0.0 reduce-scatter.2.cloned.1.call-update
  77.9 0.0 copy-done
  77.9 1.4 copy-done.1
  79.2 8.1 %fusion.2 = f32[768,2048]{1,0:T(8,128)} fusion(bf16[384,2048]{1,0:T(8,128)(2,1)S(1)} %copy-done, bf16[2048,384]{1,0:T(8,128)(2,1)S(1)} %copy-done.1, bf16[768,2048]{1,0:T(8,128)(2,1)} %all-gather.2.cloned.1.call-done, pred[768]{0:T(1024)(128)(4,1)S(1)} %iota_compare_fusion, bf16[768,384]{1,0:T(8,128)(2,1)} %param.6), kind=kOutput, calls=%fused_computation.4 | convolution fusion | flops 2418376704 | bytes 13173504 | tf_op jit(solution)/shard_map/dot_general | solution.py:36
  87.4 255.0 %all-reduce.1 = bf16[768,2048]{1,0:T(8,128)(2,1)} all-reduce(f32[768,2048]{1,0:T(8,128)} %fusion.2), channel_id=1, replica_groups=mesh['dp'=64,'rep_0'=4,'rep_1'=2] {'rep_0','rep_1'}, use_global_device_ids=true, to_apply=%region_0.1 | all-reduce | flops 1572864 | bytes 9437184 | tf_op jit(solution)/shard_map/psum | solution.py:37
  342.4 0.0 reduce-scatter.2.cloned.1.call-done
  342.4 1.4 broadcast_multiply_fusion
  (1 shorter events, 0.0 us)
Async XLA Ops:
  7.2 70.7 %copy-start = (bf16[384,2048]{1,0:T(8,128)(2,1)S(1)}, bf16[384,2048]{1,0:T(8,128)(2,1)}, u32[]{:S(2)}) copy-start(bf16[384,2048]{1,0:T(8,128)(2,1)} %param.7) | copy-start | bytes 4718596
  7.2 65.0 %all-gather.2.cloned.1.call-start = ((), (), s32[]{:S(2)}) async-start(), calls=%async_computation.1 | async-start | bytes 3932160 | tf_op jit(solution)/shard_map/all_gather | solution.py:13
  20.4 322.0 %reduce-scatter.2.cloned.1.call-start = ((), (), s32[]{:S(2)}) async-start(), calls=%async_computation.2 | async-start | bytes 3194880 | tf_op jit(solution)/shard_map/reduce_scatter | solution.py:25
  77.8 1.4 copy-start.1
Sparse Core Ops, SparseCore 0:
  20.5 51.6 all-gather.1
  78.0 225.9 reduce-scatter.1
where the time goes:
time: 351 us
  blocking collectives  268 us (76%)
  waiting for transfers between devices  51.2 us (15%)
  between operations  14.7 us (4%)
  matrix products  13.7 us (4%)
    psum x1, blocking collectives, on_device(): input_sum = lax.psum(partial_terms, REP)  255 us
    all_gather x1, waiting for transfers between devices, whole_of(): nearer = lax.all_gather(array, axes[-1], axis=dim, tiled=True)  51.1 us
    all_gather x1, blocking collectives, whole_of(): nearer = lax.all_gather(array, axes[-1], axis=dim, tiled=True)  13.1 us
    dot_general x1, matrix products, on_device(): jnp.dot(pre_grad, up_weight, preferred_element_type=jnp.float32)  8.12 us
  transfers between devices with their start and end apart: 2, of which 1 were waited for; matrix products, arithmetic and copies ran while one was open for 2% of the time, Pallas kernels for 0%

commit v1 on v0

--- a/solution.py
+++ b/solution.py
@@ -34,7 +34,7 @@
     hidden_grad = jnp.dot(grad_live, down_weight, preferred_element_type=jnp.float32)
     pre_grad = jnp.where(pre_act > 0, hidden_grad, jnp.zeros_like(hidden_grad)).astype(jnp.bfloat16)
     partial_terms = jnp.dot(pre_grad, up_weight, preferred_element_type=jnp.float32)
-    input_sum = lax.psum(partial_terms, REP)
+    input_sum = lax.psum(lax.psum(partial_terms, "rep_0"), "rep_1")
     input_grad = input_sum.astype(jnp.bfloat16)
     return (input_grad, down_grad)
 

time: 351 us -> 593 us (1.69)
  waiting for transfers between devices: 51.2 us -> 401 us
  blocking collectives: 268 us -> 161 us
    reduce_scatter x1, waiting for transfers between devices: 0.01 us -> 208 us  [on_device(): lax.psum_scatter(lax.dot_general(grad_live, hidden, (((0,), (0,)), ((), (...]
    psum x0 -> x1, waiting for transfers between devices: none -> 141 us  [on_device(): input_sum = lax.psum(lax.psum(partial_terms, 'rep_0'), 'rep_1')]
    psum x1, blocking collectives: 255 us -> 148 us  [on_device(): input_sum = lax.psum(lax.psum(partial_terms, 'rep_0'), 'rep_1')]
  transfers between devices with their start and end apart: 2 -> 3, of which waited for: 1 -> 3; matrix products, arithmetic and copies ran while one was open for 2% -> 2% of each run, Pallas kernels for 0% -> 0%
where the time goes in v1:
time: 593 us; the launch traced here: 592 us
  waiting for transfers between devices  401 us (68%)
  blocking collectives  161 us (27%)
  between operations  14.4 us (2%)
  matrix products  13.8 us (2%)
    reduce_scatter x1, waiting for transfers between devices, on_device(): lax.psum_scatter(lax.dot_general(grad_live, hidden, (((0,), (0,)), ((), (...  208 us
    psum x1, blocking collectives, on_device(): input_sum = lax.psum(lax.psum(partial_terms, 'rep_0'), 'rep_1')  148 us
    psum x1, waiting for transfers between devices, on_device(): input_sum = lax.psum(lax.psum(partial_terms, 'rep_0'), 'rep_1')  141 us
    all_gather x1, waiting for transfers between devices, whole_of(): nearer = lax.all_gather(array, axes[-1], axis=dim, tiled=True)  51.1 us
    all_gather x1, blocking collectives, whole_of(): nearer = lax.all_gather(array, axes[-1], axis=dim, tiled=True)  13.1 us
  transfers between devices with their start and end apart: 3, of which 3 were waited for; matrix products, arithmetic and copies ran while one was open for 2% of the time, Pallas kernels for 0%

profile of v1, /device:TPU:4, one launch (start us, length us, event | category | flops | bytes accessed | tf_op | source)
XLA Modules:
  0.0 592.3 jit_solution(3514502417053361099)
XLA Ops:
  7.2 0.0 copy-start
  7.2 0.0 all-gather.2.cloned.1.call-start
  7.2 13.1 %all_gather.6 = bf16[768,512]{1,0:T(8,128)(2,1)} all-gather(bf16[768,256]{1,0:T(8,128)(2,1)} %param.5), channel_id=1, replica_groups=mesh['dp'=64,'rep_0'=4,'rep_1'=2] {'rep_1'}, dimensions={1}, use_global_device_ids=true | all-gather | bytes 1179648 | tf_op jit(solution)/shard_map/all_gather | solution.py:13
  20.3 0.0 all-gather.2.cloned.1.call-update
  20.4 0.0 reduce-scatter.2.cloned.1.call-start
  21.1 51.1 %all-gather.2.cloned.1.call-done = bf16[768,2048]{1,0:T(8,128)(2,1)} async-done(((bf16[768,512]{1,0:T(8,128)(2,1)}), bf16[768,2048]{1,0:T(8,128)(2,1)}) %all-gather.2.cloned.1.call-update) | async-done | bytes 3145744 | tf_op jit(solution)/shard_map/all_gather | solution.py:13
  72.2 5.7 fusion.1
  77.9 0.0 copy-start.1
  77.9 0.0 reduce-scatter.2.cloned.1.call-update
  77.9 0.0 all-reduce.3.cloned.1.call-start
  77.9 0.0 copy-done
  77.9 1.3 copy-done.1
  79.3 8.1 %fusion.2 = f32[768,2048]{1,0:T(8,128)} fusion(bf16[384,2048]{1,0:T(8,128)(2,1)S(1)} %copy-done, bf16[2048,384]{1,0:T(8,128)(2,1)S(1)} %copy-done.1, bf16[768,2048]{1,0:T(8,128)(2,1)} %all-gather.2.cloned.1.call-done, pred[768]{0:T(1024)(128)(4,1)S(1)} %iota_compare_fusion, bf16[768,384]{1,0:T(8,128)(2,1)} %param.6), kind=kOutput, calls=%fused_computation.4 | convolution fusion | flops 2418376704 | bytes 13173504 | tf_op jit(solution)/shard_map/dot_general | solution.py:36
  87.4 0.0 all-reduce.3.cloned.1.call-update
  87.4 208.0 %reduce-scatter.2.cloned.1.call-done = f32[32,384]{1,0:T(8,128)} async-done(((f32[2048,384]{1,0:T(8,128)}), f32[32,384]{1,0:T(8,128)}) %reduce-scatter.2.cloned.1.call-update) | async-done | bytes 49168 | tf_op jit(solution)/shard_map/reduce_scatter | solution.py:25
  295.4 1.4 broadcast_multiply_fusion
  296.8 141.5 %all-reduce.3.cloned.1.call-done = f32[768,2048]{1,0:T(8,128)} async-done(((f32[768,2048]{1,0:T(8,128)}), f32[768,2048]{1,0:T(8,128)}) %all-reduce.3.cloned.1.call-update) | async-done | bytes 6291472 | tf_op jit(solution)/shard_map/psum | solution.py:37
  438.3 147.5 %all-reduce.4 = bf16[768,2048]{1,0:T(8,128)(2,1)} all-reduce(f32[768,2048]{1,0:T(8,128)} %all-reduce.3.cloned.1.call-done), channel_id=1, replica_groups=mesh['dp'=64,'rep_0'=4,'rep_1'=2] {'rep_1'}, use_global_device_ids=true, to_apply=%region_1.2 | all-reduce | flops 1572864 | bytes 9437184 | tf_op jit(solution)/shard_map/psum | solution.py:37
  (1 shorter events, 0.0 us)
Async XLA Ops:
  7.2 70.8 %copy-start = (bf16[384,2048]{1,0:T(8,128)(2,1)S(1)}, bf16[384,2048]{1,0:T(8,128)(2,1)}, u32[]{:S(2)}) copy-start(bf16[384,2048]{1,0:T(8,128)(2,1)} %param.7) | copy-start | bytes 4718596
  7.2 65.0 %all-gather.2.cloned.1.call-start = ((), (), s32[]{:S(2)}) async-start(), calls=%async_computation.1 | async-start | bytes 3932160 | tf_op jit(solution)/shard_map/all_gather | solution.py:13
  20.4 275.0 %reduce-scatter.2.cloned.1.call-start = ((), (), s32[]{:S(2)}) async-start(), calls=%async_computation.3 | async-start | bytes 3194880 | tf_op jit(solution)/shard_map/reduce_scatter | solution.py:25
  77.9 1.4 copy-start.1
  77.9 360.4 %all-reduce.3.cloned.1.call-start = ((), (), s32[]{:S(2)}) async-start(), calls=%async_computation.2 | async-start | bytes 12582912 | tf_op jit(solution)/shard_map/psum | solution.py:37
Sparse Core Ops, SparseCore 0:
  20.5 51.6 all-gather.1
  78.0 217.3 reduce-scatter.1
  297.8 140.4 all-reduce.2
